TPU v7x, 256 devices: a whole 4x4x8 slice. The times are simulated.
256 devices in a mesh: group: 16 (over x, y_lo, core), blk: 16 (over z, y_hi).
Axes of the slice: x: 4, y: 4 (y_hi: 2, y_lo: 2; y = y_hi * 2 + y_lo), z: 8, core: 2. Of those that a mesh axis runs over, the one named last changes fastest.
Arguments:
- front: float32 [16, 8192, 2048], P('group', None, 'blk'), as said below
- child_blocks: float32 [16, 16, 16, 2, 128, 128], P('group', 'blk'), may hold values from -6 to 6
- child_rows: int32 [16, 16, 16, 2, 128], P('group', 'blk'), may hold values from 2048 to 8191, as said below
- child_cols: int32 [16, 16, 16, 2, 128], P('group', 'blk'), may hold values from 0 to 127, each once within a row
- child_counts: int32 [16, 16, 16], P('group', 'blk'), may hold values from 0 to 2, as said below
Outputs:
- factors: float32 [16, 8192, 2048], P('group', None, 'blk')
- pivots: float32 [16, 256], P('group')
Inputs may be any that keep to these rules, and one draw needn't show every extreme that they name: Rows 0 to 2047 of each front form a symmetric matrix whose leading 2 * 128 rows and columns have a positive diagonal that dominates every row of that block; rows from 2048 on are unstructured. `child_rows`: the 128 row indices of one slot are distinct and lie at or below row 2048. `child_counts`: for every column block some destination group receives 2 live slots from every source group.
All inputs are finite; a program needn't handle non-finite values.
Results may differ from a plain program's by a relative error of at most 0.0003.
Values sent between devices are 32-bit elements; how exact they have to be, the bound alone decides.
A program may use at most 64 MiB of HBM per device.

v0:
```python
import jax
import jax.numpy as jnp
from jax import lax
from jax.sharding import PartitionSpec as P

PANELS = 2


def from_root(x, axis, root):
    mine = lax.axis_index(axis) == root
    return lax.psum(jnp.where(mine, x, jnp.zeros_like(x)), axis)


def factor_panel(column, start):
    size = column.shape[1]
    square = lax.slice_in_dim(column, start, start + size, axis=0)
    lower_factor = jnp.linalg.cholesky(square)
    diag_root = jnp.diagonal(lower_factor)
    solved = lax.linalg.triangular_solve(
        lower_factor, column, left_side=False, lower=True, transpose_a=True
    )
    solved = solved / diag_root
    row_ids = lax.broadcasted_iota(jnp.int32, solved.shape, 0)
    solved = jnp.where(row_ids >= start, solved, jnp.zeros_like(solved))
    return (solved, diag_root * diag_root)


def per_device(front, child_blocks, child_rows, child_cols, child_counts):
    blocks_in, rows_in, cols_in, counts_in = (
        lax.all_to_all(child_blocks, "group", split_axis=2, concat_axis=0, tiled=True),
        lax.all_to_all(child_rows, "group", split_axis=2, concat_axis=0, tiled=True),
        lax.all_to_all(child_cols, "group", split_axis=2, concat_axis=0, tiled=True),
        lax.all_to_all(child_counts, "group", split_axis=2, concat_axis=0, tiled=True),
    )
    groups = blocks_in.shape[0]
    slots = blocks_in.shape[3]
    width = blocks_in.shape[4]
    flat_blocks = blocks_in.reshape(groups * slots, width, width)
    flat_rows = rows_in.reshape(groups * slots * width)
    flat_cols = cols_in.reshape(groups * slots, width)
    slot_ids = lax.broadcasted_iota(jnp.int32, (groups, slots), 1)
    live = (slot_ids < counts_in.reshape(groups, 1)).reshape(groups * slots)
    masked = jnp.where(live[:, None, None], flat_blocks, jnp.zeros_like(flat_blocks))
    target_ids = lax.broadcasted_iota(jnp.int32, (groups * slots, width, width), 2)
    placement = (flat_cols[:, :, None] == target_ids).astype(jnp.float32)
    placed = jnp.einsum("sij,sjc->sic", masked, placement, precision=lax.Precision.HIGHEST)
    assembled = front[0].at[flat_rows].add(placed.reshape(groups * slots * width, width))
    my_index = lax.axis_index("blk")
    my_start = my_index * width
    pivot_list = []
    for panel in range(PANELS):
        start = panel * width

        def own_factor(column):
            return factor_panel(column, start)

        def empty_factor(column):
            return (jnp.zeros_like(column), jnp.zeros((width,), jnp.float32))

        factor, pivot = lax.cond(my_index == panel, own_factor, empty_factor, assembled)
        factor, pivot = (from_root(factor, "blk", panel), from_root(pivot, "blk", panel))
        my_rows = lax.dynamic_slice_in_dim(factor, my_start, width, 0)
        updated = assembled - jnp.dot(factor * pivot, my_rows.T, precision=lax.Precision.HIGHEST)
        assembled = jnp.where(
            my_index == panel, factor, jnp.where(my_index > panel, updated, assembled)
        )
        pivot_list.append(pivot)
    return (assembled[None], jnp.concatenate(pivot_list)[None])


def solution(mesh):
    in_specs = (
        P("group", None, "blk"),
        P("group", "blk", None, None, None, None),
        P("group", "blk", None, None, None),
        P("group", "blk", None, None, None),
        P("group", "blk", None),
    )
    out_specs = (P("group", None, "blk"), P("group", None))
    return jax.shard_map(
        per_device, mesh=mesh, in_specs=in_specs, out_specs=out_specs, check_vma=False
    )
```

profile of v0, /device:TPU:46, one launch (start us, length us, event | category | flops | bytes accessed | tf_op | source)
XLA Modules:
  0.0 624.9 jit_solution(7915676649362911585)
XLA Ops:
  7.2 0.0 copy-start
  7.2 0.0 copy-start.1
  7.2 4.5 copy.57
  11.7 0.0 copy-done.1
  11.7 0.1 copy.32
  11.8 8.7 %all_to_all.16 = s32[1,1,16]{1,0,2:T(1,128)S(1)} all-to-all(s32[1,1,16]{1,0,2:T(1,128)S(1)} %copy.32), channel_id=1, replica_groups=mesh['group'=16,'blk'=16] {'group'}, dimensions={2} | all-to-all | bytes 128 | tf_op jit(solution)/shard_map/all_to_all | solution.py:33
  20.4 0.0 copy-done
  20.4 8.6 %all_to_all.17 = s32[1,1,16,2,128]{4,3,1,0,2:T(2,128)S(1)} all-to-all(s32[1,1,16,2,128]{4,3,1,0,2:T(2,128)S(1)} %bitcast.54), channel_id=1, replica_groups=mesh['group'=16,'blk'=16] {'group'}, dimensions={2} | all-to-all | bytes 32768 | tf_op jit(solution)/shard_map/all_to_all | solution.py:31
  29.0 6.6 %all-to-all-start.2 = ((f32[1,1,16,2,128,128]{5,4,3,1,0,2:T(8,128)}), f32[1,1,16,2,128,128]{5,4,3,1,0,2:T(8,128)S(1)}, u32[]{:S(2)}, u32[]{:S(2)}) async-start(f32[1,1,16,2,128,128]{5,4,3,1,0,2:T(8,128)} %bitcast.50), calls=%async_computation.2 | async-start | bytes 4194304 | tf_op jit(solution)/shard_map/all_to_all | solution.py:30
  35.6 0.4 reduce.4
  36.0 0.1 iota_compare_fusion.7
  36.1 0.1 lt.45
  36.2 23.9 %all-to-all-done.2 = f32[1,1,16,2,128,128]{5,4,3,1,0,2:T(8,128)S(1)} async-done(((f32[1,1,16,2,128,128]{5,4,3,1,0,2:T(8,128)}), f32[1,1,16,2,128,128]{5,4,3,1,0,2:T(8,128)S(1)}, u32[]{:S(2)}, u32[]{:S(2)}) %all-to-all-start.2) | async-done | bytes 2097184 | tf_op jit(solution)/shard_map/all_to_all | solution.py:30
  60.1 7.9 %all-to-all-start.3 = ((s32[1,1,16,2,128]{4,3,1,0,2:T(2,128)}), s32[1,1,16,2,128]{4,3,1,0,2:T(2,128)S(1)}, u32[]{:S(2)}, u32[]{:S(2)}) async-start(s32[1,1,16,2,128]{4,3,1,0,2:T(2,128)} %bitcast.16), calls=%async_computation.3 | async-start | bytes 32768 | tf_op jit(solution)/shard_map/all_to_all | solution.py:32
  68.1 0.0 all-reduce.3.cloned.1.call-start
  68.1 1.6 bitcast_select_fusion
  69.7 1.6 all-to-all-done.3
  71.3 2.9 fusion.18
  74.2 24.3 %scatter_fusion = f32[8192,128]{1,0:T(8,128)} fusion(f32[8192,128]{1,0:T(8,128)} %bitcast.48, s32[4096]{0:T(1024)S(1)} %bitcast.51, f32[4096,128]{1,0:T(8,128)S(1)} %bitcast.49), kind=kCustom, calls=%fused_computation.2 | custom fusion | flops 524288 | bytes 6307840 | tf_op jit(solution)/shard_map/scatter-add | solution.py:47
  98.4 2.2 conditional.2
  98.4 2.2 broadcast.87.clone
  100.7 2.2 broadcast_select_fusion.1
  102.9 0.0 all-reduce.3.cloned.1.call-update
  102.9 0.0 all-reduce.5.cloned.1.call-start
  103.0 81.8 %psum.29 = f32[128]{0:T(128)S(1)} all-reduce(f32[128]{0:T(128)S(1)} %broadcast_select_fusion.3), channel_id=1, replica_groups=mesh['group'=16,'blk'=16] {'blk'}, use_global_device_ids=true, to_apply=%region_6.9 | all-reduce | flops 128 | bytes 1024 | tf_op jit(solution)/shard_map/psum | solution.py:11
  184.8 163.7 %all-reduce.3.cloned.1.call-done = f32[8192,128]{1,0:T(8,128)} async-done(((f32[8192,128]{1,0:T(8,128)}), f32[8192,128]{1,0:T(8,128)}) %all-reduce.3.cloned.1.call-update) | async-done | bytes 4194320 | tf_op jit(solution)/shard_map/psum | solution.py:11
  348.5 8.3 %fusion.11 = f32[8192,128]{1,0:T(8,128)} fusion(f32[8192,128]{1,0:T(8,128)} %all-reduce.3.cloned.1.call-done, f32[8192,128]{1,0:T(8,128)} %scatter_fusion, f32[128]{0:T(128)S(1)} %psum.29, pred[]{:T(512)S(6)} %gt.6, pred[]{:T(512)S(6)} %eq.11, s32[]{:T(128)S(6)} %select_n.89), kind=kOutput, calls=%fused_computation.33 | convolution fusion | flops 1614807040 | bytes 16843270 | tf_op jit(solution)/shard_map/dot_general | solution.py:63
  356.8 2.2 conditional.3
  356.8 2.2 broadcast.90.clone
  359.0 2.2 broadcast_select_fusion
  361.2 0.0 all-reduce.5.cloned.1.call-update
  361.3 83.9 %psum.31 = f32[128]{0:T(128)S(1)} all-reduce(f32[128]{0:T(128)S(1)} %broadcast_select_fusion.2), channel_id=1, replica_groups=mesh['group'=16,'blk'=16] {'blk'}, use_global_device_ids=true, to_apply=%region_10.13 | all-reduce | flops 128 | bytes 1024 | tf_op jit(solution)/shard_map/psum | solution.py:11
  445.2 0.6 pad_maximum_fusion
  445.7 164.0 %all-reduce.5.cloned.1.call-done = f32[8192,128]{1,0:T(8,128)} async-done(((f32[8192,128]{1,0:T(8,128)}), f32[8192,128]{1,0:T(8,128)}) %all-reduce.5.cloned.1.call-update) | async-done | bytes 4194320 | tf_op jit(solution)/shard_map/psum | solution.py:11
  609.7 8.3 %fusion.13 = f32[1,8192,128]{2,1,0:T(8,128)} fusion(f32[8192,128]{1,0:T(8,128)} %all-reduce.5.cloned.1.call-done, f32[8192,128]{1,0:T(8,128)} %fusion.11, f32[128]{0:T(128)S(1)} %psum.31, pred[]{:T(512)S(6)} %gt.7, pred[]{:T(512)S(6)} %eq.10, s32[]{:T(128)S(6)} %select_n.89), kind=kOutput, calls=%fused_computation.35 | convolution fusion | flops 1614807040 | bytes 16843270 | tf_op jit(solution)/shard_map/dot_general | solution.py:63
  (5 shorter events, 0.0 us)
Async XLA Ops:
  7.2 13.2 %copy-start = (s32[1,1,16,2,128]{4,3,2,1,0:T(2,128)S(1)}, s32[1,1,16,2,128]{4,3,2,1,0:T(2,128)}, u32[]{:S(2)}) copy-start(s32[1,1,16,2,128]{4,3,2,1,0:T(2,128)} %param.14) | copy-start | bytes 49156
  7.2 4.5 copy-start.1
  29.0 31.1 %all-to-all-start.2 = ((f32[1,1,16,2,128,128]{5,4,3,1,0,2:T(8,128)}), f32[1,1,16,2,128,128]{5,4,3,1,0,2:T(8,128)S(1)}, u32[]{:S(2)}, u32[]{:S(2)}) async-start(f32[1,1,16,2,128,128]{5,4,3,1,0,2:T(8,128)} %bitcast.50), calls=%async_computation.2 | async-start | bytes 4194304 | tf_op jit(solution)/shard_map/all_to_all | solution.py:30
  60.1 11.1 %all-to-all-start.3 = ((s32[1,1,16,2,128]{4,3,1,0,2:T(2,128)}), s32[1,1,16,2,128]{4,3,1,0,2:T(2,128)S(1)}, u32[]{:S(2)}, u32[]{:S(2)}) async-start(s32[1,1,16,2,128]{4,3,1,0,2:T(2,128)} %bitcast.16), calls=%async_computation.3 | async-start | bytes 32768 | tf_op jit(solution)/shard_map/all_to_all | solution.py:32
  68.1 280.4 %all-reduce.3.cloned.1.call-start = ((), (), s32[]{:S(2)}) async-start(), calls=%async_computation.4 | async-start | bytes 8388608 | tf_op jit(solution)/shard_map/psum | solution.py:11
  102.9 506.8 %all-reduce.5.cloned.1.call-start = ((), (), s32[]{:S(2)}) async-start(), calls=%async_computation.5 | async-start | bytes 8388608 | tf_op jit(solution)/shard_map/psum | solution.py:11
Sparse Core Ops, SparseCore 0:
  103.0 245.3 all-reduce.2
  361.4 248.3 all-reduce.4
where the time goes:
time: 629 us; the launch traced here: 625 us
  waiting for transfers between devices  353 us (56%)
  blocking collectives  183 us (29%)
  other arithmetic  31.3 us (5%)
  matrix products  19.4 us (3%)
  starting transfers between devices  14.6 us (2%)
  between operations  14.1 us (2%)
  local copies, waits for them, and re-layouts  9.16 us (1%)
    psum x2, waiting for transfers between devices, from_root(): return lax.psum(jnp.where(mine, x, jnp.zeros_like(x)), axis)  328 us
    psum x2, blocking collectives, from_root(): return lax.psum(jnp.where(mine, x, jnp.zeros_like(x)), axis)  166 us
    scatter-add x1, other arithmetic, per_device(): front[0].at[flat_rows].add(placed.reshape(groups * slots * width, width))  24.3 us
    all_to_all x1, waiting for transfers between devices, per_device(): lax.all_to_all(child_blocks, 'group', split_axis=2, concat_axis=0, tiled=...  23.9 us
    dot_general x2, matrix products, per_device(): jnp.dot(factor * pivot, my_rows.T, precision=lax.Precision.HIGHEST)  16.6 us
  transfers between devices with their start and end apart: 4, of which 4 were waited for; matrix products, arithmetic and copies ran while one was open for 0% of the time, Pallas kernels for 0%

commit v1 on v0

v1 whole, which is shorter than its diff:
```python
import functools

import jax
import jax.numpy as jnp
from jax import lax
from jax.experimental import pallas as pl
from jax.experimental.pallas import tpu as pltpu
from jax.sharding import PartitionSpec as P

MESH = pl.DeviceIdType.MESH
F32 = jnp.float32
BF16 = jnp.bfloat16
HIGHEST = lax.Precision.HIGHEST

W = 128
TOP = 2048
EARLY = TOP // 256
TSTEP = EARLY
FIRST = TSTEP + 1
BASE = 256 * FIRST
ZR = 128
YR = 256
STEP = ZR + YR


def split(x):
    hi = x.astype(BF16)
    return hi, (x - hi.astype(F32)).astype(BF16)


def remote(src, dst, send, recv, dev):
    return pltpu.make_async_remote_copy(
        src_ref=src, dst_ref=dst, send_sem=send, recv_sem=recv,
        device_id=dev, device_id_type=MESH,
    )


def kernel(
    ngroup, nblk, rows,
    front, child, cols, idx,
    out, piv,
    mb, pan, cbuf, sbuf, rbuf, hl, xw, s_ref, x_ref,
    zz_s, zz_r, zy_s, zy_r, yy_s, yy_r, back_s, ga_s, ga_r,
    in_sem, top_sem, child_sem, out_sem,
):
    g = lax.axis_index("group")
    b = lax.axis_index("blk")
    z, yh = b // 2, b % 2
    nz = nblk // 2
    other = 1 - yh
    up = {"blk": (b + 2) % nblk}
    down = {"blk": (b + nblk - 2) % nblk}
    across = {"blk": z * 2 + other}
    nlate = (rows - TOP) // STEP
    nstep = FIRST + nlate

    get_front = pltpu.make_async_copy(front, mb, in_sem)
    get_top = pltpu.make_async_copy(
        front.at[pl.ds(0, TOP)], pan.at[yh, pl.ds(0, TOP)], top_sem
    )
    get_child = pltpu.make_async_copy(child, cbuf, child_sem)
    get_child.start()

    @pl.when(z == 0)
    def _():
        get_top.start()

    get_front.start()

    barrier = pltpu.get_barrier_semaphore()
    for i in range(1, ngroup):
        pl.semaphore_signal(
            barrier, inc=1, device_id={"group": (g + i) % ngroup}, device_id_type=MESH
        )
    for dev in (up, down, across):
        pl.semaphore_signal(barrier, inc=1, device_id=dev, device_id_type=MESH)
    pl.semaphore_wait(barrier, ngroup - 1 + 3)

    def late_row(s):
        return BASE + STEP * (s - FIRST)

    def big_z(s, d, dev):
        r = pl.ds(pl.multiple_of(256 * s + 128 * d, 128), 128)
        return remote(pan.at[:, r], pan.at[:, r], zz_s.at[d, s], zz_r.at[d, s], dev)

    def late_z(s, d, dev):
        r = pl.ds(pl.multiple_of(late_row(s) + 64 * d, 64), 64)
        return remote(pan.at[:, r], pan.at[:, r], zz_s.at[d, s], zz_r.at[d, s], dev)

    def y_rows(s, d):
        start = jnp.where(s < FIRST, 256 * s, late_row(s) + ZR) + 128 * d
        return pl.ds(pl.multiple_of(start, 128), 128)

    def own_z(s, d, dev):
        r = y_rows(s, d)
        return remote(pan.at[yh, r], pan.at[yh, r], zy_s.at[d, s], zy_r.at[d, s], dev)

    def own_y(s, d):
        r = y_rows(s, d)
        return remote(pan.at[yh, r], pan.at[yh, r], yy_s.at[d, s], yy_r.at[d, s], across)

    def from_y(s, d):
        r = y_rows(s, d)
        return remote(pan.at[other, r], pan.at[other, r], yy_s.at[d, s], yy_r.at[d, s], across)

    def back(s, d, dev):
        r = y_rows(s, d)
        return remote(pan.at[other, r], pan.at[other, r], back_s.at[s], zy_r.at[d, s], dev)

    def swap(s, start, count, k):
        r = pl.ds(pl.multiple_of(start, count), count)
        return remote(pan.at[k, r], pan.at[k, r], yy_s.at[0, s], yy_r.at[0, s], across)

    def is_big(s):
        return (s == 0) | (s == TSTEP)

    def has_y(s):
        return (s != 0) & (s != TSTEP)

    def when_step(s, fn):
        pl.when((s >= 0) & (s < nstep))(fn)

    def group_copy(t):
        return remote(sbuf.at[t], rbuf.at[g], ga_s.at[t], ga_r.at[g], {"group": t})

    def group_recv(s):
        return remote(sbuf.at[s], rbuf.at[s], ga_s.at[s], ga_r.at[s], {"group": s})

    sub = lax.broadcasted_iota(jnp.int32, (W, W), 0)
    lane = lax.broadcasted_iota(jnp.int32, (W, W), 1)
    nt = (((1,), (1,)), ((), ()))
    get_child.wait()

    @pl.loop(0, ngroup)
    def _(i):
        t = (g + 1 + i) % ngroup
        for c in range(2):
            place = (cols[t, pl.ds(c, 1), :] == sub).astype(BF16)
            hi, lo = split(cbuf[t, c])
            val = lax.dot_general(hi, place, nt, preferred_element_type=F32)
            val += lax.dot_general(lo, place, nt, preferred_element_type=F32)
            sbuf[t, pl.ds(c * W, W), :] = val
        sbuf[t, pl.ds(2 * W, 8), :] = idx[t]

        @pl.when(t != g)
        def _():
            group_copy(t).start()

    def take(s, src):
        hi, lo = split(src[s, pl.ds(0, 2 * W), :])
        r = pl.ds(pl.multiple_of(s * 2 * W, 2 * W), 2 * W)
        hl[r, pl.ds(0, W)] = hi
        hl[r, pl.ds(W, W)] = lo

    def take_children():
        take(g, sbuf)
        rbuf[g, pl.ds(2 * W, 8), :] = sbuf[g, pl.ds(2 * W, 8), :]

        @pl.loop(1, ngroup)
        def _(i):
            s = (g + ngroup - i) % ngroup
            group_recv(s).wait_recv()
            take(s, rbuf)

    PER = 4

    def extend(first):
        place = lax.broadcasted_iota(jnp.int32, (STEP, W), 0).astype(F32)
        base = first.astype(F32)

        def body(q, acc):
            parts = []
            for i in range(PER):
                for c in range(2):
                    want = rbuf[q * PER + i, pl.ds(2 * W + c, 1), :] - base
                    parts.append(jnp.where(want == place, 1.0, 0.0).astype(BF16))
            hot = jnp.concatenate(parts, axis=1)
            r = pl.ds(pl.multiple_of(q * (PER * 2 * W), PER * 2 * W), PER * 2 * W)
            got = jnp.dot(hot, hl[r, :], preferred_element_type=F32)
            return acc + (got[:, :W] + got[:, W:])

        return lax.fori_loop(0, ngroup // PER, body, jnp.zeros((STEP, W), F32))

    def product(prow, count):
        x = jnp.concatenate([pan[0, pl.ds(prow, count), :], pan[1, pl.ds(prow, count), :]], axis=1)
        hi, lo = split(x)
        got = jnp.dot(hi, xw[...], preferred_element_type=F32)
        return got[:, :W] + got[:, W:] + jnp.dot(lo, xw[:, :W], preferred_element_type=F32)

    def put(first, count, n):
        r = pl.ds(first, count)
        return pltpu.make_async_copy(mb.at[r], out.at[r], out_sem.at[n])

    def set_x(x):
        hi, lo = split(x)
        xw[:, pl.ds(0, W)] = hi
        xw[:, pl.ds(W, W)] = lo

    def pivot_rows():
        res = []
        for k in range(2):
            t = pan[k, pl.ds(256 * TSTEP + W * k, W), :]
            diag = jnp.sum(jnp.where(sub == lane, t, 0.0), axis=0, keepdims=True)
            res.append(1.0 / diag)
        return res

    def top_output():
        d0, d1 = pivot_rows()
        piv[:, pl.ds(0, W)] = d0
        piv[:, pl.ds(W, W)] = d1

        @pl.when(z == 0)
        def _():
            set_x(-pan[yh, pl.ds(256 * TSTEP, 256), :])

        @pl.when(z != 0)
        def _():
            t = jnp.concatenate(
                [pan[0, pl.ds(256 * TSTEP, 256), :], pan[1, pl.ds(256 * TSTEP, 256), :]], axis=1
            )
            d = jnp.concatenate([d0, d1], axis=1)
            v = lax.dot_general(
                t, mb[pl.ds(0, 256), :], (((0,), (0,)), ((), ())),
                precision=HIGHEST, preferred_element_type=F32,
            )
            set_x(jnp.dot(t * d, v, precision=HIGHEST, preferred_element_type=F32))

        keep = jnp.where(z == 0, 0.0, 1.0).astype(F32)

        @pl.loop(0, EARLY)
        def _(e):
            r = pl.multiple_of(e * 256, 256)
            val = mb[pl.ds(r, 256), :] * keep - product(r, 256)
            row = lax.broadcasted_iota(jnp.int32, (256, W), 0) + r
            mb[pl.ds(r, 256), :] = jnp.where((row < W) & (b == 1), 0.0, val)
            put(r, 256, e).start()

    def late_output(s, extra):
        r = pl.multiple_of(TOP + STEP * (s - FIRST), 128)
        mb[pl.ds(r, STEP), :] = extra - product(pl.multiple_of(r + 256, 128), STEP)
        put(r, STEP, EARLY + s - FIRST).start()

    def eliminate():
        x_ref[...] = (sub == lane).astype(F32)

        @pl.loop(0, W)
        def _(j):
            s, x = s_ref[...], x_ref[...]
            srow, xrow = s_ref[pl.ds(j, 1), :], x_ref[pl.ds(j, 1), :]
            d = jnp.sum(jnp.where(lane[:1] == j, srow, 0.0), axis=1, keepdims=True)
            m = jnp.sum(jnp.where(lane == j, s, 0.0), axis=1, keepdims=True)
            m = jnp.where(sub[:, :1] > j, m * (1.0 / d), 0.0)
            s_ref[...] = s - m * srow
            x_ref[...] = x - m * xrow

        d = jnp.sum(jnp.where(sub == lane, s_ref[...], 0.0), axis=0, keepdims=True)
        return jnp.transpose(x_ref[...]) * (1.0 / d)

    def factor():
        dot = functools.partial(jnp.dot, precision=HIGHEST, preferred_element_type=F32)
        base = 256 * TSTEP
        a01 = pan[1, pl.ds(0, W), :]
        s_ref[...] = pan[0, pl.ds(0, W), :]
        t00 = eliminate()
        pan[0, pl.ds(base, W), :] = t00
        pan[0, pl.ds(base + W, W), :] = jnp.zeros((W, W), F32)
        back01 = dot(t00, dot(x_ref[...], a01))
        s_ref[...] = pan[1, pl.ds(W, W), :] - lax.dot_general(
            a01, back01, (((0,), (0,)), ((), ())), precision=HIGHEST, preferred_element_type=F32
        )
        t11 = eliminate()
        pan[1, pl.ds(base + W, W), :] = t11
        pan[1, pl.ds(base, W), :] = -dot(back01, t11)

    @pl.when(z == 0)
    def _():
        get_top.wait()
        swap(0, 0, 256, yh).start()

        @pl.loop(1, EARLY)
        def _(s):
            own_z(s, 0, up).start()
            own_z(s, 1, down).start()

        swap(0, 0, 256, other).wait_recv()
        big_z(0, 0, up).start()
        big_z(0, 1, down).start()
        factor()
        big_z(TSTEP, 0, up).start()
        big_z(TSTEP, 1, down).start()
        get_front.wait()
        take_children()

        @pl.loop(0, nlate + 5)
        def _(t):
            s = t + FIRST

            @pl.when(s < nstep)
            def _():
                r = pl.multiple_of(TOP + STEP * t, 128)
                val = mb[pl.ds(r, STEP), :] + extend(r)
                pan[yh, pl.ds(pl.multiple_of(r + 256, 128), STEP), :] = val
                swap(s, late_row(s), ZR, yh).start()
                own_z(s, 0, up).start()
                own_z(s, 1, down).start()
                swap(s, late_row(s), ZR, other).wait_recv()
                late_z(s, 0, up).start()
                late_z(s, 1, down).start()

            q = s - 5

            @pl.when(q == TSTEP)
            def _():
                @pl.loop(1, EARLY)
                def _(e):
                    for d in range(2):
                        back(e, d, down).wait_recv()

                top_output()

            @pl.when(q >= FIRST)
            def _():
                for d in range(2):
                    back(q, d, down).wait_recv()
                late_output(q, 0.0)

        swap(0, 0, 256, yh).wait_send()
        for s in (0, TSTEP):
            big_z(s, 0, up).wait_send()
            big_z(s, 1, down).wait_send()

        @pl.loop(1, nstep)
        def _(s):
            @pl.when(s != TSTEP)
            def _():
                own_z(s, 0, up).wait_send()
                own_z(s, 1, down).wait_send()

            @pl.when(s >= FIRST)
            def _():
                swap(s, late_row(s), ZR, yh).wait_send()
                late_z(s, 0, up).wait_send()
                late_z(s, 1, down).wait_send()

    @pl.when(z != 0)
    def _():
        lags = (z - 1, nz - 1 - z)
        devs = (up, down)
        last = (z < nz - 1, z > 1)
        lag = jnp.maximum(lags[0], lags[1]) + 2
        get_front.wait()

        @pl.loop(0, nstep + lag)
        def _(t):
            for d in range(2):
                s = t - lags[d]

                @pl.when((s >= 0) & (s < nstep))
                def _(s=s, d=d):
                    @pl.when(is_big(s))
                    def _():
                        big_z(s, d, devs[d]).wait_recv()

                        @pl.when(last[d])
                        def _():
                            big_z(s, d, devs[d]).start()

                    @pl.when(has_y(s))
                    def _():
                        own_z(s, d, devs[d]).wait_recv()
                        own_y(s, d).start()

                        @pl.when(last[d])
                        def _():
                            own_z(s, d, devs[d]).start()

                    @pl.when(s >= FIRST)
                    def _():
                        late_z(s, d, devs[d]).wait_recv()

                        @pl.when(last[d])
                        def _():
                            late_z(s, d, devs[d]).start()

            for d in range(2):
                s = t - lags[d] - 2

                @pl.when((s >= 0) & (s < nstep) & has_y(s))
                def _(s=s, d=d):
                    from_y(s, d).wait_recv()

                    @pl.when(z == (1 if d == 0 else nz - 1))
                    def _():
                        back(s, d, devs[1 - d]).start()

            s = t - lag

            @pl.when(s == TSTEP)
            def _():
                top_output()
                take_children()

            @pl.when(s >= FIRST)
            def _():
                r = pl.multiple_of(TOP + STEP * (s - FIRST), 128)
                late_output(s, mb[pl.ds(r, STEP), :] + extend(r))

        @pl.loop(0, nstep)
        def _(s):
            for d in range(2):
                @pl.when(is_big(s) & last[d])
                def _(d=d):
                    big_z(s, d, devs[d]).wait_send()

                @pl.when(has_y(s))
                def _(d=d):
                    own_y(s, d).wait_send()

                    @pl.when(last[d])
                    def _():
                        own_z(s, d, devs[d]).wait_send()

                    @pl.when(z == (1 if d == 0 else nz - 1))
                    def _():
                        back(s, d, devs[1 - d]).wait_send()

                @pl.when((s >= FIRST) & last[d])
                def _(d=d):
                    late_z(s, d, devs[d]).wait_send()

    @pl.loop(1, ngroup)
    def _(i):
        group_copy((g + i) % ngroup).wait_send()

    @pl.loop(0, EARLY)
    def _(e):
        put(pl.multiple_of(e * 256, 256), 256, e).wait()

    @pl.loop(0, nlate)
    def _(e):
        put(pl.multiple_of(TOP + e * STEP, 128), STEP, EARLY + e).wait()


def per_device(ngroup, nblk, front, child_blocks, child_rows, child_cols, child_counts):
    rows = front.shape[1]
    slots = child_blocks.shape[3]
    nstep = FIRST + (rows - TOP) // STEP
    slot = lax.broadcasted_iota(jnp.int32, (ngroup, slots), 1)
    live = slot < child_counts.reshape(ngroup, 1)
    idx = jnp.where(live[:, :, None], child_rows[0, 0], -1).astype(F32)
    idx = jnp.pad(idx, ((0, 0), (0, 8 - slots), (0, 0)), constant_values=-1.0)
    anywhere = pl.BlockSpec(memory_space=pl.ANY)
    vmem = pl.BlockSpec(memory_space=pltpu.VMEM)
    dma = pltpu.SemaphoreType.DMA
    out, piv = pl.pallas_call(
        functools.partial(kernel, ngroup, nblk, rows),
        out_shape=(
            jax.ShapeDtypeStruct((rows, W), F32),
            jax.ShapeDtypeStruct((1, 2 * W), F32),
        ),
        in_specs=[anywhere, anywhere, vmem, vmem],
        out_specs=(anywhere, vmem),
        scratch_shapes=[
            pltpu.VMEM((rows, W), F32),
            pltpu.VMEM((2, rows + 256, W), F32),
            pltpu.VMEM((ngroup, slots, W, W), F32),
            pltpu.VMEM((ngroup, slots * W + 8, W), F32),
            pltpu.VMEM((ngroup, slots * W + 8, W), F32),
            pltpu.VMEM((ngroup * slots * W, 2 * W), BF16),
            pltpu.VMEM((2 * W, 2 * W), BF16),
            pltpu.VMEM((W, W), F32),
            pltpu.VMEM((W, W), F32),
            dma((2, nstep)), dma((2, nstep)), dma((2, nstep)), dma((2, nstep)),
            dma((2, nstep)), dma((2, nstep)), dma((nstep,)),
            dma((ngroup,)), dma((ngroup,)),
            dma, dma, dma, dma((nstep,)),
        ],
        compiler_params=pltpu.CompilerParams(
            collective_id=0, has_side_effects=True, vmem_limit_bytes=48 * 2**20
        ),
        name="extend_and_factor",
    )(front[0], child_blocks[0, 0], child_cols[0, 0], idx)
    return out[None], piv


def solution(mesh):
    in_specs = (
        P("group", None, "blk"),
        P("group", "blk", None, None, None, None),
        P("group", "blk", None, None, None),
        P("group", "blk", None, None, None),
        P("group", "blk", None),
    )
    out_specs = (P("group", None, "blk"), P("group", None))
    return jax.shard_map(
        functools.partial(per_device, mesh.shape["group"], mesh.shape["blk"]),
        mesh=mesh, in_specs=in_specs, out_specs=out_specs, check_vma=False,
    )
```

time: 629 us -> 204 us (0.32)
  waiting for transfers between devices: 353 us -> 0 us
  Pallas kernels: 0 us -> 193 us
  blocking collectives: 183 us -> 0 us
  other arithmetic: 31.3 us -> 1.53 us
  matrix products: 19.4 us -> 0 us
  starting transfers between devices: 14.6 us -> 0 us
  between operations: 14.1 us -> 0.66 us
    psum x2 -> x0, waiting for transfers between devices: 328 us -> none  [from_root(): return lax.psum(jnp.where(mine, x, jnp.zeros_like(x)), axis)]
    pallas_call x0 -> x1, Pallas kernels: none -> 193 us  [per_device(): pl.pallas_call(functools.partial(kernel, ngroup, nblk, rows), out_shape=(...]
    psum x2 -> x0, blocking collectives: 166 us -> none  [from_root(): return lax.psum(jnp.where(mine, x, jnp.zeros_like(x)), axis)]
    all_to_all x2 -> x0, waiting for transfers between devices: 25.6 us -> none  [the longest x1 23.9 us: per_device(): lax.all_to_all(child_blocks, 'group', split_axis=2, concat_axis=0, tiled=...]
    scatter-add x1 -> x0, other arithmetic: 24.3 us -> none  [per_device(): front[0].at[flat_rows].add(placed.reshape(groups * slots * width, width))]
    dot_general x3 -> x0, matrix products: 19.4 us -> none  [the longest x2 16.6 us: per_device(): jnp.dot(factor * pivot, my_rows.T, precision=lax.Precision.HIGHEST)]
    all_to_all x2 -> x0, blocking collectives: 17.3 us -> none  [the longest x1 8.66 us: per_device(): lax.all_to_all(child_counts, 'group', split_axis=2, concat_axis=0, tiled=...]
    all_to_all x2 -> x0, starting transfers between devices: 14.5 us -> none  [the longest x1 7.92 us: per_device(): lax.all_to_all(child_cols, 'group', split_axis=2, concat_axis=0, tiled=True)]
  transfers between devices with their start and end apart: 4 -> 0, of which waited for: 4 -> 0; matrix products, arithmetic and copies ran while one was open for 0% -> 0% of each run, Pallas kernels for 0% -> 0%
where the time goes in v1:
time: 204 us; the launch traced here: 202 us
  Pallas kernels  193 us (95%)
  local copies, waits for them, and re-layouts  7.34 us (4%)
    pallas_call x1, Pallas kernels, per_device(): pl.pallas_call(functools.partial(kernel, ngroup, nblk, rows), out_shape=(...  193 us
    unnamed x6, local copies, waits for them, and re-layouts  7.34 us

profile of v1, /device:TPU:46, one launch (start us, length us, event | category | flops | bytes accessed | tf_op | source)
XLA Modules:
  0.0 202.2 jit_solution(8227118465259278821)
XLA Ops:
  0.6 0.7 iota_compare_fusion
  1.4 0.8 fusion
  2.2 0.0 copy-start
  2.2 1.6 copy-done
  3.8 0.0 copy-start.1
  3.8 0.7 copy-done.1
  4.5 192.7 %extend_and_factor.1 = (f32[8192,128]{1,0:T(8,128)}, f32[1,256]{1,0:T(1,128)S(1)}) custom-call(f32[8192,128]{1,0:T(8,128)} %bitcast.11, f32[16,2,128,128]{3,2,1,0:T(8,128)S(1)} %bitcast.9, s32[16,2,128]{2,1,0:T(2,128)S(1)} %bitcast.10, f32[16,8,128]{2,1,0:T(8,128)S(1)} %pad.4.idx), custom_call_target="tpu_custom_call" | custom-call | tf_op jit(solution)/shard_map/extend_and_factor/pallas_call | solution.py:455
  197.2 4.5 %copy.9 = f32[1,8192,128]{2,1,0:T(8,128)} copy(f32[1,8192,128]{2,1,0:T(8,128)} %bitcast.12) | data formatting | bytes 8388608
  201.7 0.6 copy.10
  (1 shorter events, 0.0 us)
Async XLA Ops:
  2.2 1.6 copy-start
  3.8 0.7 copy-start.1

commit v2 on v1

--- a/solution.py
+++ b/solution.py
@@ -18,9 +18,13 @@
 TSTEP = EARLY
 FIRST = TSTEP + 1
 BASE = 256 * FIRST
-ZR = 128
-YR = 256
+ZR = 64
+YR = 128
 STEP = ZR + YR
+PAIR = 2 * STEP
+HOP = 3
+CROSS = 3
+EVERY = 4
 
 
 def split(x):
@@ -84,27 +88,29 @@
         return remote(pan.at[:, r], pan.at[:, r], zz_s.at[d, s], zz_r.at[d, s], dev)
 
     def late_z(s, d, dev):
-        r = pl.ds(pl.multiple_of(late_row(s) + 64 * d, 64), 64)
+        r = pl.ds(pl.multiple_of(late_row(s) + ZR // 2 * d, ZR // 2), ZR // 2)
         return remote(pan.at[:, r], pan.at[:, r], zz_s.at[d, s], zz_r.at[d, s], dev)
 
-    def y_rows(s, d):
-        start = jnp.where(s < FIRST, 256 * s, late_row(s) + ZR) + 128 * d
-        return pl.ds(pl.multiple_of(start, 128), 128)
-
-    def own_z(s, d, dev):
-        r = y_rows(s, d)
+    def y_rows(s, d, early):
+        if early:
+            return pl.ds(pl.multiple_of(256 * s + 128 * d, 128), 128)
+        half = YR // 2
+        return pl.ds(pl.multiple_of(late_row(s) + ZR + half * d, half), half)
+
+    def own_z(s, d, dev, early):
+        r = y_rows(s, d, early)
         return remote(pan.at[yh, r], pan.at[yh, r], zy_s.at[d, s], zy_r.at[d, s], dev)
 
-    def own_y(s, d):
-        r = y_rows(s, d)
+    def own_y(s, d, early):
+        r = y_rows(s, d, early)
         return remote(pan.at[yh, r], pan.at[yh, r], yy_s.at[d, s], yy_r.at[d, s], across)
 
-    def from_y(s, d):
-        r = y_rows(s, d)
+    def from_y(s, d, early):
+        r = y_rows(s, d, early)
         return remote(pan.at[other, r], pan.at[other, r], yy_s.at[d, s], yy_r.at[d, s], across)
 
-    def back(s, d, dev):
-        r = y_rows(s, d)
+    def back(s, d, dev, early):
+        r = y_rows(s, d, early)
         return remote(pan.at[other, r], pan.at[other, r], back_s.at[s], zy_r.at[d, s], dev)
 
     def swap(s, start, count, k):
@@ -114,11 +120,11 @@
     def is_big(s):
         return (s == 0) | (s == TSTEP)
 
-    def has_y(s):
-        return (s != 0) & (s != TSTEP)
-
-    def when_step(s, fn):
-        pl.when((s >= 0) & (s < nstep))(fn)
+    def is_early(s):
+        return (s >= 1) & (s < TSTEP)
+
+    def is_late(s):
+        return (s >= FIRST) & (s < nstep)
 
     def group_copy(t):
         return remote(sbuf.at[t], rbuf.at[g], ga_s.at[t], ga_r.at[g], {"group": t})
@@ -129,10 +135,8 @@
     sub = lax.broadcasted_iota(jnp.int32, (W, W), 0)
     lane = lax.broadcasted_iota(jnp.int32, (W, W), 1)
     nt = (((1,), (1,)), ((), ()))
-    get_child.wait()
-
-    @pl.loop(0, ngroup)
-    def _(i):
+
+    def give(i):
         t = (g + 1 + i) % ngroup
         for c in range(2):
             place = (cols[t, pl.ds(c, 1), :] == sub).astype(BF16)
@@ -152,20 +156,23 @@
         hl[r, pl.ds(0, W)] = hi
         hl[r, pl.ds(W, W)] = lo
 
-    def take_children():
-        take(g, sbuf)
-        rbuf[g, pl.ds(2 * W, 8), :] = sbuf[g, pl.ds(2 * W, 8), :]
-
-        @pl.loop(1, ngroup)
-        def _(i):
-            s = (g + ngroup - i) % ngroup
+    def take_child(i):
+        s = (g + ngroup - i) % ngroup
+
+        @pl.when(i == 0)
+        def _():
+            take(g, sbuf)
+            rbuf[g, pl.ds(2 * W, 8), :] = sbuf[g, pl.ds(2 * W, 8), :]
+
+        @pl.when(i > 0)
+        def _():
             group_recv(s).wait_recv()
             take(s, rbuf)
 
-    PER = 4
+    PER = 8
 
     def extend(first):
-        place = lax.broadcasted_iota(jnp.int32, (STEP, W), 0).astype(F32)
+        place = lax.broadcasted_iota(jnp.int32, (PAIR, W), 0).astype(F32)
         base = first.astype(F32)
 
         def body(q, acc):
@@ -179,7 +186,7 @@
             got = jnp.dot(hot, hl[r, :], preferred_element_type=F32)
             return acc + (got[:, :W] + got[:, W:])
 
-        return lax.fori_loop(0, ngroup // PER, body, jnp.zeros((STEP, W), F32))
+        return lax.fori_loop(0, ngroup // PER, body, jnp.zeros((PAIR, W), F32))
 
     def product(prow, count):
         x = jnp.concatenate([pan[0, pl.ds(prow, count), :], pan[1, pl.ds(prow, count), :]], axis=1)
@@ -204,7 +211,7 @@
             res.append(1.0 / diag)
         return res
 
-    def top_output():
+    def top_factor():
         d0, d1 = pivot_rows()
         piv[:, pl.ds(0, W)] = d0
         piv[:, pl.ds(W, W)] = d1
@@ -225,20 +232,18 @@
             )
             set_x(jnp.dot(t * d, v, precision=HIGHEST, preferred_element_type=F32))
 
+    def top_output(e):
         keep = jnp.where(z == 0, 0.0, 1.0).astype(F32)
-
-        @pl.loop(0, EARLY)
-        def _(e):
-            r = pl.multiple_of(e * 256, 256)
-            val = mb[pl.ds(r, 256), :] * keep - product(r, 256)
-            row = lax.broadcasted_iota(jnp.int32, (256, W), 0) + r
-            mb[pl.ds(r, 256), :] = jnp.where((row < W) & (b == 1), 0.0, val)
-            put(r, 256, e).start()
-
-    def late_output(s, extra):
-        r = pl.multiple_of(TOP + STEP * (s - FIRST), 128)
-        mb[pl.ds(r, STEP), :] = extra - product(pl.multiple_of(r + 256, 128), STEP)
-        put(r, STEP, EARLY + s - FIRST).start()
+        r = pl.multiple_of(e * 256, 256)
+        val = mb[pl.ds(r, 256), :] * keep - product(r, 256)
+        row = lax.broadcasted_iota(jnp.int32, (256, W), 0) + r
+        mb[pl.ds(r, 256), :] = jnp.where((row < W) & (b == 1), 0.0, val)
+        put(r, 256, e).start()
+
+    def late_output(u, extra):
+        r = pl.multiple_of(TOP + PAIR * u, 128)
+        mb[pl.ds(r, PAIR), :] = extra - product(pl.multiple_of(r + 256, 128), PAIR)
+        put(r, PAIR, EARLY + u).start()
 
     def eliminate():
         x_ref[...] = (sub == lane).astype(F32)
@@ -247,9 +252,10 @@
         def _(j):
             s, x = s_ref[...], x_ref[...]
             srow, xrow = s_ref[pl.ds(j, 1), :], x_ref[pl.ds(j, 1), :]
-            d = jnp.sum(jnp.where(lane[:1] == j, srow, 0.0), axis=1, keepdims=True)
-            m = jnp.sum(jnp.where(lane == j, s, 0.0), axis=1, keepdims=True)
-            m = jnp.where(sub[:, :1] > j, m * (1.0 / d), 0.0)
+            at = jnp.full((W, W), j, jnp.int32)
+            m = jnp.take_along_axis(s, at, axis=1)
+            d = jnp.take_along_axis(jnp.broadcast_to(srow, (8, W)), at[:8], axis=1)[:1]
+            m = jnp.where(sub > j, m * (1.0 / d), 0.0)
             s_ref[...] = s - m * srow
             x_ref[...] = x - m * xrow
 
@@ -276,157 +282,200 @@
     def _():
         get_top.wait()
         swap(0, 0, 256, yh).start()
-
-        @pl.loop(1, EARLY)
-        def _(s):
-            own_z(s, 0, up).start()
-            own_z(s, 1, down).start()
-
-        swap(0, 0, 256, other).wait_recv()
-        big_z(0, 0, up).start()
-        big_z(0, 1, down).start()
+        get_child.wait()
+
+        @pl.loop(0, ngroup)
+        def _(i):
+            give(i)
+
+            @pl.when(i == 3)
+            def _():
+                swap(0, 0, 256, other).wait_recv()
+                big_z(0, 0, up).start()
+                big_z(0, 1, down).start()
+
+            @pl.when((i > 3) & (i < 3 + EARLY))
+            def _():
+                own_z(i - 3, 0, up, True).start()
+                own_z(i - 3, 1, down, True).start()
+
         factor()
         big_z(TSTEP, 0, up).start()
         big_z(TSTEP, 1, down).start()
         get_front.wait()
-        take_children()
-
-        @pl.loop(0, nlate + 5)
-        def _(t):
-            s = t + FIRST
-
-            @pl.when(s < nstep)
-            def _():
-                r = pl.multiple_of(TOP + STEP * t, 128)
-                val = mb[pl.ds(r, STEP), :] + extend(r)
-                pan[yh, pl.ds(pl.multiple_of(r + 256, 128), STEP), :] = val
-                swap(s, late_row(s), ZR, yh).start()
-                own_z(s, 0, up).start()
-                own_z(s, 1, down).start()
-                swap(s, late_row(s), ZR, other).wait_recv()
-                late_z(s, 0, up).start()
-                late_z(s, 1, down).start()
-
-            q = s - 5
-
-            @pl.when(q == TSTEP)
-            def _():
-                @pl.loop(1, EARLY)
-                def _(e):
-                    for d in range(2):
-                        back(e, d, down).wait_recv()
-
-                top_output()
-
-            @pl.when(q >= FIRST)
-            def _():
+        pl.loop(0, ngroup)(take_child)
+
+        def own_send(s):
+            swap(s, late_row(s), ZR, yh).start()
+            own_z(s, 0, up, False).start()
+            own_z(s, 1, down, False).start()
+
+        def both_send(s):
+            swap(s, late_row(s), ZR, other).wait_recv()
+            late_z(s, 0, up).start()
+            late_z(s, 1, down).start()
+
+        @pl.loop(0, nlate // 2)
+        def _(u):
+            r = pl.multiple_of(TOP + PAIR * u, 128)
+            val = mb[pl.ds(r, PAIR), :] + extend(r)
+            pan[yh, pl.ds(pl.multiple_of(r + 256, 128), PAIR), :] = val
+            s = FIRST + 2 * u
+            own_send(s)
+            own_send(s + 1)
+
+            @pl.when(u > 0)
+            def _():
+                both_send(s - 2)
+                both_send(s - 1)
+
+        both_send(nstep - 2)
+        both_send(nstep - 1)
+        top_factor()
+        top_output(0)
+
+        @pl.loop(0, nlate // 2)
+        def _(u):
+            for i in range(2):
                 for d in range(2):
-                    back(q, d, down).wait_recv()
-                late_output(q, 0.0)
+                    back(FIRST + 2 * u + i, d, down, False).wait_recv()
+            late_output(u, 0.0)
+
+        @pl.loop(1, EARLY)
+        def _(e):
+            for d in range(2):
+                back(e, d, down, True).wait_recv()
+            top_output(e)
 
         swap(0, 0, 256, yh).wait_send()
         for s in (0, TSTEP):
             big_z(s, 0, up).wait_send()
             big_z(s, 1, down).wait_send()
 
-        @pl.loop(1, nstep)
+        @pl.loop(1, EARLY)
         def _(s):
-            @pl.when(s != TSTEP)
-            def _():
-                own_z(s, 0, up).wait_send()
-                own_z(s, 1, down).wait_send()
-
-            @pl.when(s >= FIRST)
-            def _():
-                swap(s, late_row(s), ZR, yh).wait_send()
-                late_z(s, 0, up).wait_send()
-                late_z(s, 1, down).wait_send()
+            own_z(s, 0, up, True).wait_send()
+            own_z(s, 1, down, True).wait_send()
+
+        @pl.loop(FIRST, nstep)
+        def _(s):
+            own_z(s, 0, up, False).wait_send()
+            own_z(s, 1, down, False).wait_send()
+            swap(s, late_row(s), ZR, yh).wait_send()
+            late_z(s, 0, up).wait_send()
+            late_z(s, 1, down).wait_send()
 
     @pl.when(z != 0)
     def _():
-        lags = (z - 1, nz - 1 - z)
+        lags = (HOP * (z - 1), HOP * (nz - 1 - z))
         devs = (up, down)
         last = (z < nz - 1, z > 1)
-        lag = jnp.maximum(lags[0], lags[1]) + 2
+        turn = (z == 1, z == nz - 1)
+        lag = HOP * (nz - 2) + CROSS
+        get_child.wait()
+        pl.loop(0, ngroup)(give)
         get_front.wait()
+
+        def crossing(s):
+            n = s - FIRST
+            return jnp.where((n > 0) & (n % EVERY == 0) & (n < EVERY * EARLY), n // EVERY, 0)
 
         @pl.loop(0, nstep + lag)
         def _(t):
             for d in range(2):
                 s = t - lags[d]
-
-                @pl.when((s >= 0) & (s < nstep))
+                e = crossing(s)
+
+                @pl.when(is_big(s))
                 def _(s=s, d=d):
-                    @pl.when(is_big(s))
+                    big_z(s, d, devs[d]).wait_recv()
+
+                    @pl.when(last[d])
                     def _():
-                        big_z(s, d, devs[d]).wait_recv()
+                        big_z(s, d, devs[d]).start()
+
+                for early, cond in ((True, is_early(s)), (False, is_late(s))):
+                    @pl.when(cond)
+                    def _(s=s, d=d, early=early):
+                        own_z(s, d, devs[d], early).wait_recv()
 
                         @pl.when(last[d])
                         def _():
-                            big_z(s, d, devs[d]).start()
-
-                    @pl.when(has_y(s))
-                    def _():
-                        own_z(s, d, devs[d]).wait_recv()
-                        own_y(s, d).start()
-
-                        @pl.when(last[d])
-                        def _():
-                            own_z(s, d, devs[d]).start()
-
-                    @pl.when(s >= FIRST)
-                    def _():
-                        late_z(s, d, devs[d]).wait_recv()
-
-                        @pl.when(last[d])
-                        def _():
-                            late_z(s, d, devs[d]).start()
+                            own_z(s, d, devs[d], early).start()
+
+                        if not early:
+                            own_y(s, d, early).start()
+
+                @pl.when(e > 0)
+                def _(e=e, d=d):
+                    own_y(e, d, True).start()
 
             for d in range(2):
-                s = t - lags[d] - 2
-
-                @pl.when((s >= 0) & (s < nstep) & has_y(s))
+                s = t - lags[d] - CROSS
+                e = crossing(s)
+
+                @pl.when(is_late(s))
                 def _(s=s, d=d):
-                    from_y(s, d).wait_recv()
-
-                    @pl.when(z == (1 if d == 0 else nz - 1))
-                    def _():
-                        back(s, d, devs[1 - d]).start()
-
-            s = t - lag
-
-            @pl.when(s == TSTEP)
-            def _():
-                top_output()
-                take_children()
-
-            @pl.when(s >= FIRST)
-            def _():
-                r = pl.multiple_of(TOP + STEP * (s - FIRST), 128)
-                late_output(s, mb[pl.ds(r, STEP), :] + extend(r))
-
-        @pl.loop(0, nstep)
-        def _(s):
-            for d in range(2):
-                @pl.when(is_big(s) & last[d])
-                def _(d=d):
-                    big_z(s, d, devs[d]).wait_send()
-
-                @pl.when(has_y(s))
-                def _(d=d):
-                    own_y(s, d).wait_send()
+                    late_z(s, d, devs[d]).wait_recv()
 
                     @pl.when(last[d])
                     def _():
-                        own_z(s, d, devs[d]).wait_send()
-
-                    @pl.when(z == (1 if d == 0 else nz - 1))
-                    def _():
-                        back(s, d, devs[1 - d]).wait_send()
-
-                @pl.when((s >= FIRST) & last[d])
+                        late_z(s, d, devs[d]).start()
+
+                for early, q, cond in ((False, s, is_late(s)), (True, e, e > 0)):
+                    @pl.when(cond)
+                    def _(q=q, d=d, early=early):
+                        from_y(q, d, early).wait_recv()
+
+                        @pl.when(turn[d])
+                        def _():
+                            back(q, d, devs[1 - d], early).start()
+
+            s = t - lag
+            n = s - FIRST
+
+            @pl.when((n >= -8) & (n < 0))
+            def _():
+                take_child(2 * (n + 8))
+                take_child(2 * (n + 8) + 1)
+
+            @pl.when(s == TSTEP)
+            def _():
+                top_factor()
+                top_output(0)
+
+            @pl.when(crossing(s) > 0)
+            def _():
+                top_output(crossing(s))
+
+            @pl.when((n > 0) & (n % 2 == 1))
+            def _():
+                u = n // 2
+                r = pl.multiple_of(TOP + PAIR * u, 128)
+                late_output(u, mb[pl.ds(r, PAIR), :] + extend(r))
+
+        for s in (0, TSTEP):
+            for d in range(2):
+                @pl.when(last[d])
+                def _(s=s, d=d):
+                    big_z(s, d, devs[d]).wait_send()
+
+        def drain(s, early):
+            for d in range(2):
+                own_y(s, d, early).wait_send()
+
+                @pl.when(last[d])
                 def _(d=d):
-                    late_z(s, d, devs[d]).wait_send()
+                    own_z(s, d, devs[d], early).wait_send()
+                    if not early:
+                        late_z(s, d, devs[d]).wait_send()
+
+                @pl.when(turn[d])
+                def _(d=d):
+                    back(s, d, devs[1 - d], early).wait_send()
+
+        pl.loop(1, EARLY)(lambda s: drain(s, True))
+        pl.loop(FIRST, nstep)(lambda s: drain(s, False))
 
     @pl.loop(1, ngroup)
     def _(i):
@@ -436,9 +485,9 @@
     def _(e):
         put(pl.multiple_of(e * 256, 256), 256, e).wait()
 
-    @pl.loop(0, nlate)
-    def _(e):
-        put(pl.multiple_of(TOP + e * STEP, 128), STEP, EARLY + e).wait()
+    @pl.loop(0, nlate // 2)
+    def _(u):
+        put(pl.multiple_of(TOP + u * PAIR, 128), PAIR, EARLY + u).wait()
 
 
 def per_device(ngroup, nblk, front, child_blocks, child_rows, child_cols, child_counts):

time: 204 us -> 163 us (0.80)
  Pallas kernels: 193 us -> 153 us
    pallas_call x1, Pallas kernels: 193 us -> 153 us  [per_device(): pl.pallas_call(functools.partial(kernel, ngroup, nblk, rows), out_shape=(...]
where the time goes in v2:
time: 163 us
  Pallas kernels  153 us (94%)
  local copies, waits for them, and re-layouts  7.34 us (5%)
    pallas_call x1, Pallas kernels, per_device(): pl.pallas_call(functools.partial(kernel, ngroup, nblk, rows), out_shape=(...  153 us
    unnamed x6, local copies, waits for them, and re-layouts  7.34 us

profile of v2, /device:TPU:46, one launch (start us, length us, event | category | flops | bytes accessed | tf_op | source)
XLA Modules:
  0.0 162.8 jit_solution(9679959611659230124)
XLA Ops:
  0.6 0.7 iota_compare_fusion
  1.4 0.8 fusion
  2.2 0.0 copy-start
  2.2 1.6 copy-done
  3.8 0.0 copy-start.1
  3.8 0.7 copy-done.1
  4.5 153.2 %extend_and_factor.1 = (f32[8192,128]{1,0:T(8,128)}, f32[1,256]{1,0:T(1,128)S(1)}) custom-call(f32[8192,128]{1,0:T(8,128)} %bitcast.11, f32[16,2,128,128]{3,2,1,0:T(8,128)S(1)} %bitcast.9, s32[16,2,128]{2,1,0:T(2,128)S(1)} %bitcast.10, f32[16,8,128]{2,1,0:T(8,128)S(1)} %pad.4.idx), custom_call_target="tpu_custom_call" | custom-call | tf_op jit(solution)/shard_map/extend_and_factor/pallas_call | solution.py:504
  157.7 4.5 %copy.9 = f32[1,8192,128]{2,1,0:T(8,128)} copy(f32[1,8192,128]{2,1,0:T(8,128)} %bitcast.12) | data formatting | bytes 8388608
  162.2 0.6 copy.10
  (1 shorter events, 0.0 us)
Async XLA Ops:
  2.2 1.6 copy-start
  3.8 0.7 copy-start.1

commit v3 on v2

--- a/solution.py
+++ b/solution.py
@@ -41,9 +41,9 @@
 
 def kernel(
     ngroup, nblk, rows,
-    front, child, cols, idx,
+    front, child, child_rows, cols, counts,
     out, piv,
-    mb, pan, cbuf, sbuf, rbuf, hl, xw, s_ref, x_ref,
+    mb, pan, sbuf, rbuf, hl, xw, s_ref, x_ref,
     zz_s, zz_r, zy_s, zy_r, yy_s, yy_r, back_s, ga_s, ga_r,
     in_sem, top_sem, child_sem, out_sem,
 ):
@@ -62,7 +62,7 @@
     get_top = pltpu.make_async_copy(
         front.at[pl.ds(0, TOP)], pan.at[yh, pl.ds(0, TOP)], top_sem
     )
-    get_child = pltpu.make_async_copy(child, cbuf, child_sem)
+    get_child = pltpu.make_async_copy(child, sbuf.at[:, pl.ds(0, 2 * W)], child_sem)
     get_child.start()
 
     @pl.when(z == 0)
@@ -70,6 +70,13 @@
         get_top.start()
 
     get_front.start()
+
+    @pl.loop(0, ngroup)
+    def _(t):
+        slot = lax.broadcasted_iota(jnp.int32, (2, W), 0)
+        at = jnp.where(slot < counts[0, t], child_rows[t], -1)
+        sbuf[t, pl.ds(2 * W, 2), :] = at.astype(F32)
+        sbuf[t, pl.ds(2 * W + 2, 2), :] = cols[t].astype(F32)
 
     barrier = pltpu.get_barrier_semaphore()
     for i in range(1, ngroup):
@@ -85,11 +92,11 @@
 
     def big_z(s, d, dev):
         r = pl.ds(pl.multiple_of(256 * s + 128 * d, 128), 128)
-        return remote(pan.at[:, r], pan.at[:, r], zz_s.at[d, s], zz_r.at[d, s], dev)
+        return remote(pan.at[:, r], pan.at[:, r], zz_s.at[d], zz_r.at[d, s], dev)
 
     def late_z(s, d, dev):
         r = pl.ds(pl.multiple_of(late_row(s) + ZR // 2 * d, ZR // 2), ZR // 2)
-        return remote(pan.at[:, r], pan.at[:, r], zz_s.at[d, s], zz_r.at[d, s], dev)
+        return remote(pan.at[:, r], pan.at[:, r], zz_s.at[d], zz_r.at[d, s], dev)
 
     def y_rows(s, d, early):
         if early:
@@ -99,23 +106,32 @@
 
     def own_z(s, d, dev, early):
         r = y_rows(s, d, early)
-        return remote(pan.at[yh, r], pan.at[yh, r], zy_s.at[d, s], zy_r.at[d, s], dev)
+        return remote(pan.at[yh, r], pan.at[yh, r], zy_s.at[d], zy_r.at[d, s], dev)
 
     def own_y(s, d, early):
         r = y_rows(s, d, early)
-        return remote(pan.at[yh, r], pan.at[yh, r], yy_s.at[d, s], yy_r.at[d, s], across)
+        return remote(pan.at[yh, r], pan.at[yh, r], yy_s.at[d], yy_r.at[d, s], across)
 
     def from_y(s, d, early):
         r = y_rows(s, d, early)
-        return remote(pan.at[other, r], pan.at[other, r], yy_s.at[d, s], yy_r.at[d, s], across)
+        return remote(pan.at[other, r], pan.at[other, r], yy_s.at[d], yy_r.at[d, s], across)
 
     def back(s, d, dev, early):
         r = y_rows(s, d, early)
-        return remote(pan.at[other, r], pan.at[other, r], back_s.at[s], zy_r.at[d, s], dev)
+        return remote(pan.at[other, r], pan.at[other, r], back_s, zy_r.at[d, s], dev)
 
     def swap(s, start, count, k):
         r = pl.ds(pl.multiple_of(start, count), count)
-        return remote(pan.at[k, r], pan.at[k, r], yy_s.at[0, s], yy_r.at[0, s], across)
+        return remote(pan.at[k, r], pan.at[k, r], yy_s.at[0], yy_r.at[0, s], across)
+
+    own_rows = (EARLY - 1) * W + nlate * (YR // 2)
+
+    def sent_z(d):
+        dev = (up, down)[d]
+        own = pan.at[yh, pl.ds(0, own_rows)]
+        remote(own, own, zy_s.at[d], zy_r.at[d, 0], dev).wait_send()
+        both = pan.at[:, pl.ds(0, 2 * W + nlate * (ZR // 2))]
+        remote(both, both, zz_s.at[d], zz_r.at[d, 0], dev).wait_send()
 
     def is_big(s):
         return (s == 0) | (s == TSTEP)
@@ -127,10 +143,10 @@
         return (s >= FIRST) & (s < nstep)
 
     def group_copy(t):
-        return remote(sbuf.at[t], rbuf.at[g], ga_s.at[t], ga_r.at[g], {"group": t})
+        return remote(sbuf.at[t], rbuf.at[g], ga_s, ga_r.at[g], {"group": t})
 
     def group_recv(s):
-        return remote(sbuf.at[s], rbuf.at[s], ga_s.at[s], ga_r.at[s], {"group": s})
+        return remote(sbuf.at[s], rbuf.at[s], ga_s, ga_r.at[s], {"group": s})
 
     sub = lax.broadcasted_iota(jnp.int32, (W, W), 0)
     lane = lax.broadcasted_iota(jnp.int32, (W, W), 1)
@@ -138,23 +154,19 @@
 
     def give(i):
         t = (g + 1 + i) % ngroup
-        for c in range(2):
-            place = (cols[t, pl.ds(c, 1), :] == sub).astype(BF16)
-            hi, lo = split(cbuf[t, c])
-            val = lax.dot_general(hi, place, nt, preferred_element_type=F32)
-            val += lax.dot_general(lo, place, nt, preferred_element_type=F32)
-            sbuf[t, pl.ds(c * W, W), :] = val
-        sbuf[t, pl.ds(2 * W, 8), :] = idx[t]
 
         @pl.when(t != g)
         def _():
             group_copy(t).start()
 
     def take(s, src):
-        hi, lo = split(src[s, pl.ds(0, 2 * W), :])
-        r = pl.ds(pl.multiple_of(s * 2 * W, 2 * W), 2 * W)
-        hl[r, pl.ds(0, W)] = hi
-        hl[r, pl.ds(W, W)] = lo
+        for c in range(2):
+            place = (src[s, pl.ds(2 * W + 2 + c, 1), :] == sub.astype(F32)).astype(BF16)
+            both = jnp.concatenate(split(src[s, pl.ds(c * W, W), :]), axis=0)
+            got = lax.dot_general(both, place, nt, preferred_element_type=F32).astype(BF16)
+            r = pl.ds(pl.multiple_of(s * 2 * W + c * W, W), W)
+            hl[r, pl.ds(0, W)] = got[:W]
+            hl[r, pl.ds(W, W)] = got[W:]
 
     def take_child(i):
         s = (g + ngroup - i) % ngroup
@@ -248,16 +260,19 @@
     def eliminate():
         x_ref[...] = (sub == lane).astype(F32)
 
-        @pl.loop(0, W)
-        def _(j):
-            s, x = s_ref[...], x_ref[...]
-            srow, xrow = s_ref[pl.ds(j, 1), :], x_ref[pl.ds(j, 1), :]
-            at = jnp.full((W, W), j, jnp.int32)
-            m = jnp.take_along_axis(s, at, axis=1)
-            d = jnp.take_along_axis(jnp.broadcast_to(srow, (8, W)), at[:8], axis=1)[:1]
-            m = jnp.where(sub > j, m * (1.0 / d), 0.0)
-            s_ref[...] = s - m * srow
-            x_ref[...] = x - m * xrow
+        for lo in range(0, W, 32):
+            rest = pl.ds(lo, W - lo)
+
+            @pl.loop(lo, lo + 32)
+            def _(j):
+                s, x = s_ref[rest, :], x_ref[rest, :]
+                srow, xrow = s_ref[pl.ds(j, 1), :], x_ref[pl.ds(j, 1), :]
+                at = jnp.full((W - lo, W), j, jnp.int32)
+                m = jnp.take_along_axis(s, at, axis=1)
+                d = jnp.take_along_axis(jnp.broadcast_to(srow, (8, W)), at[:8], axis=1)[:1]
+                m = jnp.where(sub[lo:] > j, m * (1.0 / d), 0.0)
+                s_ref[rest, :] = s - m * srow
+                x_ref[rest, :] = x - m * xrow
 
         d = jnp.sum(jnp.where(sub == lane, s_ref[...], 0.0), axis=0, keepdims=True)
         return jnp.transpose(x_ref[...]) * (1.0 / d)
@@ -347,23 +362,10 @@
                 back(e, d, down, True).wait_recv()
             top_output(e)
 
-        swap(0, 0, 256, yh).wait_send()
-        for s in (0, TSTEP):
-            big_z(s, 0, up).wait_send()
-            big_z(s, 1, down).wait_send()
-
-        @pl.loop(1, EARLY)
-        def _(s):
-            own_z(s, 0, up, True).wait_send()
-            own_z(s, 1, down, True).wait_send()
-
-        @pl.loop(FIRST, nstep)
-        def _(s):
-            own_z(s, 0, up, False).wait_send()
-            own_z(s, 1, down, False).wait_send()
-            swap(s, late_row(s), ZR, yh).wait_send()
-            late_z(s, 0, up).wait_send()
-            late_z(s, 1, down).wait_send()
+        swapped = pan.at[yh, pl.ds(0, 256 + nlate * ZR)]
+        remote(swapped, swapped, yy_s.at[0], yy_r.at[0, 0], across).wait_send()
+        for d in range(2):
+            sent_z(d)
 
     @pl.when(z != 0)
     def _():
@@ -384,7 +386,6 @@
         def _(t):
             for d in range(2):
                 s = t - lags[d]
-                e = crossing(s)
 
                 @pl.when(is_big(s))
                 def _(s=s, d=d):
@@ -403,12 +404,7 @@
                         def _():
                             own_z(s, d, devs[d], early).start()
 
-                        if not early:
-                            own_y(s, d, early).start()
-
-                @pl.when(e > 0)
-                def _(e=e, d=d):
-                    own_y(e, d, True).start()
+                        own_y(s, d, early).start()
 
             for d in range(2):
                 s = t - lags[d] - CROSS
@@ -454,32 +450,18 @@
                 r = pl.multiple_of(TOP + PAIR * u, 128)
                 late_output(u, mb[pl.ds(r, PAIR), :] + extend(r))
 
-        for s in (0, TSTEP):
-            for d in range(2):
-                @pl.when(last[d])
-                def _(s=s, d=d):
-                    big_z(s, d, devs[d]).wait_send()
-
-        def drain(s, early):
-            for d in range(2):
-                own_y(s, d, early).wait_send()
-
-                @pl.when(last[d])
-                def _(d=d):
-                    own_z(s, d, devs[d], early).wait_send()
-                    if not early:
-                        late_z(s, d, devs[d]).wait_send()
-
-                @pl.when(turn[d])
-                def _(d=d):
-                    back(s, d, devs[1 - d], early).wait_send()
-
-        pl.loop(1, EARLY)(lambda s: drain(s, True))
-        pl.loop(FIRST, nstep)(lambda s: drain(s, False))
-
-    @pl.loop(1, ngroup)
-    def _(i):
-        group_copy((g + i) % ngroup).wait_send()
+        for d in range(2):
+            own = pan.at[yh, pl.ds(0, own_rows)]
+            remote(own, own, yy_s.at[d], yy_r.at[d, 0], across).wait_send()
+            pl.when(last[d])(functools.partial(sent_z, d))
+
+        @pl.when((z == 1) | (z == nz - 1))
+        def _():
+            own = pan.at[yh, pl.ds(0, own_rows)]
+            remote(own, own, back_s, zy_r.at[0, 0], up).wait_send()
+
+    given = sbuf.at[pl.ds(0, ngroup - 1)]
+    remote(given, given, ga_s, ga_r.at[0], {"group": (g + 1) % ngroup}).wait_send()
 
     @pl.loop(0, EARLY)
     def _(e):
@@ -494,12 +476,9 @@
     rows = front.shape[1]
     slots = child_blocks.shape[3]
     nstep = FIRST + (rows - TOP) // STEP
-    slot = lax.broadcasted_iota(jnp.int32, (ngroup, slots), 1)
-    live = slot < child_counts.reshape(ngroup, 1)
-    idx = jnp.where(live[:, :, None], child_rows[0, 0], -1).astype(F32)
-    idx = jnp.pad(idx, ((0, 0), (0, 8 - slots), (0, 0)), constant_values=-1.0)
-    anywhere = pl.BlockSpec(memory_space=pl.ANY)
+    hbm = pl.BlockSpec(memory_space=pltpu.HBM)
     vmem = pl.BlockSpec(memory_space=pltpu.VMEM)
+    smem = pl.BlockSpec(memory_space=pltpu.SMEM)
     dma = pltpu.SemaphoreType.DMA
     out, piv = pl.pallas_call(
         functools.partial(kernel, ngroup, nblk, rows),
@@ -507,28 +486,30 @@
             jax.ShapeDtypeStruct((rows, W), F32),
             jax.ShapeDtypeStruct((1, 2 * W), F32),
         ),
-        in_specs=[anywhere, anywhere, vmem, vmem],
-        out_specs=(anywhere, vmem),
+        in_specs=[hbm, hbm, vmem, vmem, smem],
+        out_specs=(hbm, vmem),
         scratch_shapes=[
             pltpu.VMEM((rows, W), F32),
             pltpu.VMEM((2, rows + 256, W), F32),
-            pltpu.VMEM((ngroup, slots, W, W), F32),
             pltpu.VMEM((ngroup, slots * W + 8, W), F32),
             pltpu.VMEM((ngroup, slots * W + 8, W), F32),
             pltpu.VMEM((ngroup * slots * W, 2 * W), BF16),
             pltpu.VMEM((2 * W, 2 * W), BF16),
             pltpu.VMEM((W, W), F32),
             pltpu.VMEM((W, W), F32),
-            dma((2, nstep)), dma((2, nstep)), dma((2, nstep)), dma((2, nstep)),
-            dma((2, nstep)), dma((2, nstep)), dma((nstep,)),
-            dma((ngroup,)), dma((ngroup,)),
+            dma((2,)), dma((2, nstep)), dma((2,)), dma((2, nstep)),
+            dma((2,)), dma((2, nstep)), dma,
+            dma, dma((ngroup,)),
             dma, dma, dma, dma((nstep,)),
         ],
         compiler_params=pltpu.CompilerParams(
-            collective_id=0, has_side_effects=True, vmem_limit_bytes=48 * 2**20
+            collective_id=0, has_side_effects=True, vmem_limit_bytes=56 * 2**20
         ),
         name="extend_and_factor",
-    )(front[0], child_blocks[0, 0], child_cols[0, 0], idx)
+    )(
+        front[0], child_blocks.reshape(ngroup, slots * W, W), child_rows[0, 0],
+        child_cols[0, 0], child_counts.reshape(1, ngroup),
+    )
     return out[None], piv
 
 

time: 163 us -> 142 us (0.87)
  Pallas kernels: 153 us -> 136 us
  local copies, waits for them, and re-layouts: 7.34 us -> 5.04 us
    pallas_call x1, Pallas kernels: 153 us -> 136 us  [per_device(): pl.pallas_call(functools.partial(kernel, ngroup, nblk, rows), out_shape=(...]
    unnamed x6 -> x4, local copies, waits for them, and re-layouts: 7.34 us -> 5.04 us
where the time goes in v3:
time: 142 us
  Pallas kernels  136 us (96%)
  local copies, waits for them, and re-layouts  5.04 us (4%)
    pallas_call x1, Pallas kernels, per_device(): pl.pallas_call(functools.partial(kernel, ngroup, nblk, rows), out_shape=(...  136 us
    unnamed x4, local copies, waits for them, and re-layouts  5.04 us

profile of v3, /device:TPU:46, one launch (start us, length us, event | category | flops | bytes accessed | tf_op | source)
XLA Modules:
  0.0 141.9 jit_solution(17244016438965118517)
XLA Ops:
  0.6 136.2 %extend_and_factor.1 = (f32[8192,128]{1,0:T(8,128)}, f32[1,256]{1,0:T(1,128)}) custom-call(f32[8192,128]{1,0:T(8,128)} %bitcast.6, f32[16,256,128]{2,1,0:T(8,128)} %bitcast.8, s32[16,2,128]{2,1,0:T(2,128)} %bitcast.9, s32[16,2,128]{2,1,0:T(2,128)} %bitcast.10, s32[1,16]{1,0:T(1,128)} %bitcast.11), custom_call_target="tpu_custom_call" | custom-call | tf_op jit(solution)/shard_map/extend_and_factor/pallas_call | solution.py:483
  136.8 0.0 copy-start
  136.8 4.5 %copy.9 = f32[1,8192,128]{2,1,0:T(8,128)} copy(f32[1,8192,128]{2,1,0:T(8,128)} %bitcast.7) | data formatting | bytes 8388608
  141.3 0.0 copy-done
  141.3 0.6 copy.10
Async XLA Ops:
  136.8 4.5 %copy-start = (f32[1,256]{1,0:T(1,128)S(1)}, f32[1,256]{1,0:T(1,128)}, u32[]{:S(2)}) copy-start(f32[1,256]{1,0:T(1,128)} %get-tuple-element.9) | copy-start | bytes 3076

commit v4 on v3

--- a/solution.py
+++ b/solution.py
@@ -23,7 +23,7 @@
 STEP = ZR + YR
 PAIR = 2 * STEP
 HOP = 3
-CROSS = 3
+CROSS = 4
 EVERY = 4
 
 
@@ -181,7 +181,7 @@
             group_recv(s).wait_recv()
             take(s, rbuf)
 
-    PER = 8
+    PER = 16
 
     def extend(first):
         place = lax.broadcasted_iota(jnp.int32, (PAIR, W), 0).astype(F32)

time: 142 us -> 137 us (0.965)
  Pallas kernels: 136 us -> 131 us
    pallas_call x1, Pallas kernels: 136 us -> 131 us  [per_device(): pl.pallas_call(functools.partial(kernel, ngroup, nblk, rows), out_shape=(...]
where the time goes in v4:
time: 137 us; the launch traced here: 136 us
  Pallas kernels  131 us (96%)
  local copies, waits for them, and re-layouts  5.04 us (4%)
    pallas_call x1, Pallas kernels, per_device(): pl.pallas_call(functools.partial(kernel, ngroup, nblk, rows), out_shape=(...  131 us
    unnamed x4, local copies, waits for them, and re-layouts  5.04 us

profile of v4, /device:TPU:46, one launch (start us, length us, event | category | flops | bytes accessed | tf_op | source)
XLA Modules:
  0.0 136.4 jit_solution(5430450550248887382)
XLA Ops:
  0.6 130.7 %extend_and_factor.1 = (f32[8192,128]{1,0:T(8,128)}, f32[1,256]{1,0:T(1,128)}) custom-call(f32[8192,128]{1,0:T(8,128)} %bitcast.6, f32[16,256,128]{2,1,0:T(8,128)} %bitcast.8, s32[16,2,128]{2,1,0:T(2,128)} %bitcast.9, s32[16,2,128]{2,1,0:T(2,128)} %bitcast.10, s32[1,16]{1,0:T(1,128)} %bitcast.11), custom_call_target="tpu_custom_call" | custom-call | tf_op jit(solution)/shard_map/extend_and_factor/pallas_call | solution.py:483
  131.4 0.0 copy-start
  131.4 4.5 %copy.9 = f32[1,8192,128]{2,1,0:T(8,128)} copy(f32[1,8192,128]{2,1,0:T(8,128)} %bitcast.7) | data formatting | bytes 8388608
  135.8 0.0 copy-done
  135.8 0.6 copy.10
Async XLA Ops:
  131.4 4.5 %copy-start = (f32[1,256]{1,0:T(1,128)S(1)}, f32[1,256]{1,0:T(1,128)}, u32[]{:S(2)}) copy-start(f32[1,256]{1,0:T(1,128)} %get-tuple-element.9) | copy-start | bytes 3076

commit v5 on v4

--- a/solution.py
+++ b/solution.py
@@ -24,6 +24,7 @@
 PAIR = 2 * STEP
 HOP = 3
 CROSS = 4
+AHEAD = 8
 EVERY = 4
 
 
@@ -181,24 +182,19 @@
             group_recv(s).wait_recv()
             take(s, rbuf)
 
-    PER = 16
-
-    def extend(first):
+    def extend(first, lo, count):
         place = lax.broadcasted_iota(jnp.int32, (PAIR, W), 0).astype(F32)
         base = first.astype(F32)
-
-        def body(q, acc):
-            parts = []
-            for i in range(PER):
-                for c in range(2):
-                    want = rbuf[q * PER + i, pl.ds(2 * W + c, 1), :] - base
-                    parts.append(jnp.where(want == place, 1.0, 0.0).astype(BF16))
-            hot = jnp.concatenate(parts, axis=1)
-            r = pl.ds(pl.multiple_of(q * (PER * 2 * W), PER * 2 * W), PER * 2 * W)
-            got = jnp.dot(hot, hl[r, :], preferred_element_type=F32)
-            return acc + (got[:, :W] + got[:, W:])
-
-        return lax.fori_loop(0, ngroup // PER, body, jnp.zeros((PAIR, W), F32))
+        parts = []
+        for i in range(lo, lo + count):
+            for c in range(2):
+                want = rbuf[i, pl.ds(2 * W + c, 1), :] - base
+                parts.append(jnp.where(want == place, 1.0, 0.0).astype(BF16))
+        hot = jnp.concatenate(parts, axis=1)
+        got = jnp.dot(
+            hot, hl[pl.ds(lo * 2 * W, count * 2 * W), :], preferred_element_type=F32
+        )
+        return got[:, :W] + got[:, W:]
 
     def product(prow, count):
         x = jnp.concatenate([pan[0, pl.ds(prow, count), :], pan[1, pl.ds(prow, count), :]], axis=1)
@@ -333,7 +329,7 @@
         @pl.loop(0, nlate // 2)
         def _(u):
             r = pl.multiple_of(TOP + PAIR * u, 128)
-            val = mb[pl.ds(r, PAIR), :] + extend(r)
+            val = mb[pl.ds(r, PAIR), :] + extend(r, 0, ngroup)
             pan[yh, pl.ds(pl.multiple_of(r + 256, 128), PAIR), :] = val
             s = FIRST + 2 * u
             own_send(s)
@@ -430,10 +426,12 @@
             s = t - lag
             n = s - FIRST
 
-            @pl.when((n >= -8) & (n < 0))
-            def _():
-                take_child(2 * (n + 8))
-                take_child(2 * (n + 8) + 1)
+            m = n + AHEAD
+
+            @pl.when((m >= -8) & (m < 0))
+            def _():
+                take_child(2 * (m + 8))
+                take_child(2 * (m + 8) + 1)
 
             @pl.when(s == TSTEP)
             def _():
@@ -444,11 +442,24 @@
             def _():
                 top_output(crossing(s))
 
+            half = ngroup // 2
+
+            @pl.when((m >= 0) & (m < nlate))
+            def _():
+                r = pl.multiple_of(TOP + PAIR * (m // 2), 128)
+
+                @pl.when(m % 2 == 0)
+                def _():
+                    mb[pl.ds(r, PAIR), :] += extend(r, 0, half)
+
+                @pl.when(m % 2 == 1)
+                def _():
+                    mb[pl.ds(r, PAIR), :] += extend(r, half, half)
+
             @pl.when((n > 0) & (n % 2 == 1))
             def _():
                 u = n // 2
-                r = pl.multiple_of(TOP + PAIR * u, 128)
-                late_output(u, mb[pl.ds(r, PAIR), :] + extend(r))
+                late_output(u, mb[pl.ds(pl.multiple_of(TOP + PAIR * u, 128), PAIR), :])
 
         for d in range(2):
             own = pan.at[yh, pl.ds(0, own_rows)]

time: 137 us -> 135 us (0.985)
  Pallas kernels: 131 us -> 129 us
    pallas_call x1, Pallas kernels: 131 us -> 129 us  [per_device(): pl.pallas_call(functools.partial(kernel, ngroup, nblk, rows), out_shape=(...]
where the time goes in v5:
time: 135 us
  Pallas kernels  129 us (96%)
  local copies, waits for them, and re-layouts  5.04 us (4%)
    pallas_call x1, Pallas kernels, per_device(): pl.pallas_call(functools.partial(kernel, ngroup, nblk, rows), out_shape=(...  129 us
    unnamed x4, local copies, waits for them, and re-layouts  5.04 us

profile of v5, /device:TPU:46, one launch (start us, length us, event | category | flops | bytes accessed | tf_op | source)
XLA Modules:
  0.0 134.8 jit_solution(14672230286707462907)
XLA Ops:
  0.6 129.1 %extend_and_factor.1 = (f32[8192,128]{1,0:T(8,128)}, f32[1,256]{1,0:T(1,128)}) custom-call(f32[8192,128]{1,0:T(8,128)} %bitcast.6, f32[16,256,128]{2,1,0:T(8,128)} %bitcast.8, s32[16,2,128]{2,1,0:T(2,128)} %bitcast.9, s32[16,2,128]{2,1,0:T(2,128)} %bitcast.10, s32[1,16]{1,0:T(1,128)} %bitcast.11), custom_call_target="tpu_custom_call" | custom-call | tf_op jit(solution)/shard_map/extend_and_factor/pallas_call | solution.py:494
  129.8 0.0 copy-start
  129.8 4.5 %copy.9 = f32[1,8192,128]{2,1,0:T(8,128)} copy(f32[1,8192,128]{2,1,0:T(8,128)} %bitcast.7) | data formatting | bytes 8388608
  134.2 0.0 copy-done
  134.2 0.6 copy.10
Async XLA Ops:
  129.8 4.5 %copy-start = (f32[1,256]{1,0:T(1,128)S(1)}, f32[1,256]{1,0:T(1,128)}, u32[]{:S(2)}) copy-start(f32[1,256]{1,0:T(1,128)} %get-tuple-element.9) | copy-start | bytes 3076

commit v6 on v5

--- a/solution.py
+++ b/solution.py
@@ -153,12 +153,15 @@
     lane = lax.broadcasted_iota(jnp.int32, (W, W), 1)
     nt = (((1,), (1,)), ((), ()))
 
+    def partner(i, sign):
+        n = (7 * i) % ngroup
+        core = (g + n) % 2
+        y = (g // 2 + n // 2) % 2
+        x = (g // 4 + sign * (n // 4) + ngroup // 4) % (ngroup // 4)
+        return x * 4 + y * 2 + core
+
     def give(i):
-        t = (g + 1 + i) % ngroup
-
-        @pl.when(t != g)
-        def _():
-            group_copy(t).start()
+        group_copy(partner(i, 1)).start()
 
     def take(s, src):
         for c in range(2):
@@ -170,7 +173,7 @@
             hl[r, pl.ds(W, W)] = got[W:]
 
     def take_child(i):
-        s = (g + ngroup - i) % ngroup
+        s = partner(i, -1)
 
         @pl.when(i == 0)
         def _():
@@ -297,7 +300,7 @@
 
         @pl.loop(0, ngroup)
         def _(i):
-            give(i)
+            pl.when(i > 0)(functools.partial(give, i))
 
             @pl.when(i == 3)
             def _():
@@ -371,7 +374,7 @@
         turn = (z == 1, z == nz - 1)
         lag = HOP * (nz - 2) + CROSS
         get_child.wait()
-        pl.loop(0, ngroup)(give)
+        pl.loop(1, ngroup)(give)
         get_front.wait()
 
         def crossing(s):

time: 135 us -> 134 us (level)
  Pallas kernels: 129 us -> 127 us
    pallas_call x1, Pallas kernels: 129 us -> 127 us  [per_device(): pl.pallas_call(functools.partial(kernel, ngroup, nblk, rows), out_shape=(...]
where the time goes in v6:
time: 134 us; the launch traced here: 133 us
  Pallas kernels  127 us (95%)
  local copies, waits for them, and re-layouts  5.04 us (4%)
    pallas_call x1, Pallas kernels, per_device(): pl.pallas_call(functools.partial(kernel, ngroup, nblk, rows), out_shape=(...  127 us
    unnamed x4, local copies, waits for them, and re-layouts  5.04 us

profile of v6, /device:TPU:46, one launch (start us, length us, event | category | flops | bytes accessed | tf_op | source)
XLA Modules:
  0.0 132.8 jit_solution(4878551773325332399)
XLA Ops:
  0.6 127.1 %extend_and_factor.1 = (f32[8192,128]{1,0:T(8,128)}, f32[1,256]{1,0:T(1,128)}) custom-call(f32[8192,128]{1,0:T(8,128)} %bitcast.6, f32[16,256,128]{2,1,0:T(8,128)} %bitcast.8, s32[16,2,128]{2,1,0:T(2,128)} %bitcast.9, s32[16,2,128]{2,1,0:T(2,128)} %bitcast.10, s32[1,16]{1,0:T(1,128)} %bitcast.11), custom_call_target="tpu_custom_call" | custom-call | tf_op jit(solution)/shard_map/extend_and_factor/pallas_call | solution.py:497
  127.7 0.0 copy-start
  127.7 4.5 %copy.9 = f32[1,8192,128]{2,1,0:T(8,128)} copy(f32[1,8192,128]{2,1,0:T(8,128)} %bitcast.7) | data formatting | bytes 8388608
  132.2 0.0 copy-done
  132.2 0.6 copy.10
Async XLA Ops:
  127.7 4.5 %copy-start = (f32[1,256]{1,0:T(1,128)S(1)}, f32[1,256]{1,0:T(1,128)}, u32[]{:S(2)}) copy-start(f32[1,256]{1,0:T(1,128)} %get-tuple-element.9) | copy-start | bytes 3076
